TPU v7x, 32 devices: a whole 2x2x4 slice. The times are simulated.
32 devices in a mesh: ctx: 2 (over x), head: 4 (over y, core), rep: 4 (over z).
Axes of the slice: x: 2, y: 2, z: 4, core: 2. Of those that a mesh axis runs over, the one named last changes fastest.
Arguments:
- tokens: bfloat16 [4, 256, 4096], P('rep', 'ctx'), may hold values from -6 to 6
- queries: bfloat16 [4, 256, 4096], P('rep', 'ctx', 'head'), may hold values from -40 to 40
- cotangent: bfloat16 [4, 256, 4096], P('rep', 'ctx', 'head'), may hold values from -0.19921875 to 0.19921875
- key_weight: bfloat16 [4096, 1024], P('ctx', 'head'), may hold values from -0.09375 to 0.09375
- value_weight: bfloat16 [4096, 1024], P('ctx', 'head'), may hold values from -0.09375 to 0.09375
- probe: int32 [2, 4096, 1024], P(None, None, 'head'), may hold values from -1 to 1, as said below
Outputs:
- curvature: float32 [2, 4096, 1024], P(None, 'ctx', 'head')
Inputs may be any that keep to these rules, and one draw needn't show every extreme that they name: `probe`: every entry is -1 or 1.
All inputs are finite; a program needn't handle non-finite values.
Results may differ from a plain program's by a relative error of at most 0.0095.
The roundings to bfloat16 on the way count: a program that leaves them out, or rounds other values in their place, can miss the bound.
Values may be sent and summed in bfloat16 or wider, within the bound.
A program may use at most 128 MiB of HBM per device.

v0:
```python
import jax
import jax.numpy as jnp
from jax import lax
from jax.sharding import PartitionSpec as P

HEADS = 32
KV_HEADS = 8
HEAD_DIM = 128


NEG_FILL = -1e30


def times_t(left, right):
    return lax.dot_general(
        left, right, (((1,), (1,)), ((), ())), preferred_element_type=jnp.float32
    )


def times_tn(left, right):
    return lax.dot_general(
        left, right, (((0,), (0,)), ((), ())), preferred_element_type=jnp.float32
    )


def head_rows(block, head_index, group):
    width = group * HEAD_DIM
    return block[:, head_index * width : (head_index + 1) * width].reshape(-1, HEAD_DIM)


def forward_stats(query_rows, cot_rows, head_context, query_start, block, block_count, group):
    scaling = HEAD_DIM ** (-0.5)
    keys, values, tan_keys, tan_values = head_context
    row_count = query_rows.shape[0]
    query_pos = query_start + jnp.arange(row_count, dtype=jnp.int32) // group

    def masked_scores(block_index):
        offset = block_index * block
        key_block = lax.dynamic_slice_in_dim(keys, offset, block, 0)
        key_pos = offset + jnp.arange(block, dtype=jnp.int32)
        valid = key_pos[None, :] <= query_pos[:, None]
        return (jnp.where(valid, scaling * times_t(query_rows, key_block), NEG_FILL), offset)

    def peak_step(block_index, peak):
        scores, offset = masked_scores(block_index)
        return jnp.maximum(peak, jnp.max(scores, axis=1))

    peak = lax.fori_loop(0, block_count, peak_step, jnp.full((row_count,), NEG_FILL, jnp.float32))

    def accumulate(block_index, carry):
        total, along, acc_value, acc_mixed, acc_tan = carry
        scores, offset = masked_scores(block_index)
        tan_scores = scaling * times_t(
            query_rows, lax.dynamic_slice_in_dim(tan_keys, offset, block, 0)
        )
        value_block = lax.dynamic_slice_in_dim(values, offset, block, 0)
        tan_value_block = lax.dynamic_slice_in_dim(tan_values, offset, block, 0)
        expo = jnp.exp(scores - peak[:, None])
        expo_half = expo.astype(jnp.bfloat16)
        total = total + jnp.sum(expo, axis=1)
        along = along + jnp.sum(expo * tan_scores, axis=1)
        acc_value = acc_value + jnp.dot(expo_half, value_block, preferred_element_type=jnp.float32)
        acc_mixed = acc_mixed + jnp.dot(
            (expo * tan_scores).astype(jnp.bfloat16),
            value_block,
            preferred_element_type=jnp.float32,
        )
        acc_tan = acc_tan + jnp.dot(expo_half, tan_value_block, preferred_element_type=jnp.float32)
        return (total, along, acc_value, acc_mixed, acc_tan)

    row_zero = jnp.zeros((row_count,), jnp.float32)
    block_zero = jnp.zeros((row_count, HEAD_DIM), jnp.float32)
    total, along, acc_value, acc_mixed, acc_tan = lax.fori_loop(
        0, block_count, accumulate, (row_zero, row_zero, block_zero, block_zero, block_zero)
    )
    output = acc_value / total[:, None]
    shift_mean = along / total
    tan_output = (acc_mixed - shift_mean[:, None] * acc_value) / total[:, None] + acc_tan / total[
        :, None
    ]
    cot_float = cot_rows.astype(jnp.float32)
    delta = jnp.sum(cot_float * output, axis=1)
    tan_delta = jnp.sum(cot_float * tan_output, axis=1)
    return (peak, total, shift_mean, delta, tan_delta)


def pair_terms(query_block, cot_block, stats, query_start, kv_block, key_start, group, local_kv):
    scaling = HEAD_DIM ** (-0.5)
    query_count = query_block.shape[0]
    key_count = kv_block[0].shape[0]

    def compute():
        key_parts = []
        value_parts = []
        for head_index in range(local_kv):
            columns = slice(head_index * HEAD_DIM, (head_index + 1) * HEAD_DIM)
            keys = kv_block[0][:, columns]
            values = kv_block[1][:, columns]
            tan_keys = kv_block[2][:, columns]
            tan_values = kv_block[3][:, columns]
            query_rows = head_rows(query_block, head_index, group)
            cot_rows = head_rows(cot_block, head_index, group)
            peak, total, shift_mean, delta, tan_delta = tuple(
                (
                    item[:, head_index * group : (head_index + 1) * group].reshape(-1)
                    for item in stats
                )
            )
            query_pos = query_start + jnp.arange(query_count * group, dtype=jnp.int32) // group
            key_pos = jnp.arange(key_count, dtype=jnp.int32)
            valid = key_pos[None, :] <= query_pos[:, None]
            scores = jnp.where(valid, scaling * times_t(query_rows, keys), NEG_FILL)
            tan_scores = scaling * times_t(query_rows, tan_keys)
            probs = jnp.exp(scores - peak[:, None]) / total[:, None]
            tan_probs = probs * (tan_scores - shift_mean[:, None])
            value_parts.append(times_tn(tan_probs.astype(jnp.bfloat16), cot_rows))
            dprob = times_t(cot_rows, values)
            tan_dprob = times_t(cot_rows, tan_values)
            tan_dscore = tan_probs * (dprob - delta[:, None]) + probs * (
                tan_dprob - tan_delta[:, None]
            )
            key_parts.append(scaling * times_tn(tan_dscore.astype(jnp.bfloat16), query_rows))
        return jnp.concatenate(key_parts + value_parts, axis=1)

    def nothing():
        return jnp.zeros((key_count, 2 * local_kv * HEAD_DIM), jnp.float32)

    return lax.cond(key_start <= query_start + query_count - 1, compute, nothing)


def local(tokens, queries, cotangent, key_weight, value_weight, probe):
    tok = tokens[0]
    query_local = queries[0]
    cot_local = cotangent[0]
    tok_rows = tok.shape[0]
    model_dim = tok.shape[1]
    width = key_weight.shape[1]
    local_kv = width // HEAD_DIM
    group = HEADS // KV_HEADS
    sign = probe.astype(jnp.float32).astype(jnp.bfloat16)
    ctx_size = lax.axis_size("ctx")
    position = lax.axis_index("ctx")
    columns = tok
    sign_key = sign[0]
    sign_value = sign[1]
    projected = (
        jnp.dot(
            columns,
            lax.all_gather(key_weight, "ctx", axis=0, tiled=True),
            preferred_element_type=jnp.float32,
        ),
        jnp.dot(
            columns,
            lax.all_gather(value_weight, "ctx", axis=0, tiled=True),
            preferred_element_type=jnp.float32,
        ),
        jnp.dot(columns, sign_key, preferred_element_type=jnp.float32),
        jnp.dot(columns, sign_value, preferred_element_type=jnp.float32),
    )
    own_keys, own_values, own_tan_keys, own_tan_values = tuple(
        (item.astype(jnp.bfloat16) for item in projected)
    )
    context = (
        lax.all_gather(own_keys, "ctx", axis=0, tiled=True),
        lax.all_gather(own_values, "ctx", axis=0, tiled=True),
        lax.all_gather(own_tan_keys, "ctx", axis=0, tiled=True),
        lax.all_gather(own_tan_values, "ctx", axis=0, tiled=True),
    )
    per_block = 1
    while per_block * 2 <= max(1, 512 // tok_rows) and ctx_size % (per_block * 2) == 0:
        per_block = per_block * 2
    block = per_block * tok_rows
    query_start = position * tok_rows
    block_count = (query_start + tok_rows - 1) // block + 1
    stat_lists = ([], [], [], [], [])
    for head_index in range(local_kv):
        head_context = tuple(
            (item[:, head_index * HEAD_DIM : (head_index + 1) * HEAD_DIM] for item in context)
        )
        results = forward_stats(
            head_rows(query_local, head_index, group),
            head_rows(cot_local, head_index, group),
            head_context,
            query_start,
            block,
            block_count,
            group,
        )
        for member in range(5):
            stat_lists[member].append(results[member].reshape(tok_rows, group))
    stat_peak, stat_total, stat_shift, stat_delta, stat_tan_delta = tuple(
        (jnp.concatenate(items, axis=1) for items in stat_lists)
    )
    stats = (stat_peak, stat_total, stat_shift, stat_delta, stat_tan_delta)
    kv_block = tuple((item for item in context))
    terms = lax.psum_scatter(
        pair_terms(
            query_local, cot_local, stats, query_start, kv_block, jnp.int32(0), group, local_kv
        ),
        "ctx",
        scatter_dimension=0,
        tiled=True,
    )
    grads = terms.astype(jnp.bfloat16)
    own_rows = model_dim // ctx_size
    columns = tok
    partial_hvp = lax.psum_scatter(times_tn(columns, grads), "ctx", scatter_dimension=0, tiled=True)
    hvp = lax.psum(partial_hvp, "rep")
    hvp = hvp.reshape(own_rows, 2, width).transpose(1, 0, 2)
    sign_rows = lax.dynamic_slice_in_dim(probe, position * own_rows, own_rows, 1).astype(
        jnp.float32
    )
    return sign_rows * hvp


def solution(mesh):
    return jax.shard_map(
        local,
        mesh=mesh,
        in_specs=(
            P("rep", "ctx", None),
            P("rep", "ctx", "head"),
            P("rep", "ctx", "head"),
            P("ctx", "head"),
            P("ctx", "head"),
            P(None, None, "head"),
        ),
        out_specs=P(None, "ctx", "head"),
        check_vma=False,
    )
```

profile of v0, /device:TPU:0, one launch (start us, length us, event | category | flops | bytes accessed | tf_op | source)
XLA Modules:
  0.0 396.3 jit_solution(134997586182628034)
XLA Ops:
  6.5 0.7 all-gather.5.cloned.1.call-update
  7.3 0.7 all-gather.3.cloned.1.call-update
  8.1 1.0 fusion.106
  9.2 4.1 %convert_convert_fusion = bf16[2,4096,256]{2,1,0:T(8,128)(2,1)S(1)} fusion(s32[2,4096,256]{2,1,0:T(8,128)} %param.21), kind=kLoop, calls=%fused_computation.134 | loop fusion | flops 4194304 | bytes 12582912 | tf_op jit(solution)/shard_map/convert_element_type | solution.py:140
  13.3 0.5 fusion.92
  13.8 5.8 %all_gather.20 = bf16[256,256]{1,0:T(8,128)(2,1)S(1)} all-gather(bf16[128,256]{1,0:T(8,128)(2,1)S(1)} %fusion.92), channel_id=1, replica_groups=mesh['ctx'=2,'head'=4,'rep'=4] {'ctx'}, dimensions={0}, use_global_device_ids=true | all-gather | bytes 196608 | tf_op jit(solution)/shard_map/all_gather | solution.py:166
  19.6 0.5 fusion.93
  20.1 6.3 %all_gather.23 = bf16[256,256]{1,0:T(8,128)(2,1)S(1)} all-gather(bf16[128,256]{1,0:T(8,128)(2,1)S(1)} %fusion.93), channel_id=1, replica_groups=mesh['ctx'=2,'head'=4,'rep'=4] {'ctx'}, dimensions={0}, use_global_device_ids=true | all-gather | bytes 196608 | tf_op jit(solution)/shard_map/all_gather | solution.py:167
  26.5 19.7 %all-gather.5.cloned.1.call-done = bf16[4096,256]{1,0:T(8,128)(2,1)} async-done(((bf16[2048,256]{1,0:T(8,128)(2,1)}), bf16[4096,256]{1,0:T(8,128)(2,1)}) %all-gather.5.cloned.1.call-update) | async-done | bytes 2097168 | tf_op jit(solution)/shard_map/all_gather | solution.py:154
  46.2 2.0 convolution_convert_fusion
  48.2 4.9 %all_gather.22 = bf16[256,256]{1,0:T(8,128)(2,1)S(1)} all-gather(bf16[128,256]{1,0:T(8,128)(2,1)S(1)} %convolution_convert_fusion), channel_id=1, replica_groups=mesh['ctx'=2,'head'=4,'rep'=4] {'ctx'}, dimensions={0}, use_global_device_ids=true | all-gather | bytes 196608 | tf_op jit(solution)/shard_map/all_gather | solution.py:165
  53.1 27.7 %all-gather.3.cloned.1.call-done = bf16[4096,256]{1,0:T(8,128)(2,1)} async-done(((bf16[2048,256]{1,0:T(8,128)(2,1)}), bf16[4096,256]{1,0:T(8,128)(2,1)}) %all-gather.3.cloned.1.call-update) | async-done | bytes 2097168 | tf_op jit(solution)/shard_map/all_gather | solution.py:149
  80.8 2.0 convolution_convert_fusion.1
  82.9 4.9 %all_gather.19 = bf16[256,256]{1,0:T(8,128)(2,1)S(1)} all-gather(bf16[128,256]{1,0:T(8,128)(2,1)S(1)} %convolution_convert_fusion.1), channel_id=1, replica_groups=mesh['ctx'=2,'head'=4,'rep'=4] {'ctx'}, dimensions={0}, use_global_device_ids=true | all-gather | bytes 196608 | tf_op jit(solution)/shard_map/all_gather | solution.py:164
  88.9 1.5 while.63
  90.5 1.5 while.61
  92.0 10.9 %conditional.1 = (f32[256,512]{0,1:T(8,128)S(1)}) conditional(s32[]{:T(128)} %convert_element_type.76, () %tuple.37, (s32[]{:T(128)}, bf16[128,1024]{1,0:T(8,128)(2,1)}, bf16[256,256]{1,0:T(8,128)(2,1)}, f32[512]{0:T(512)S(1)}, f32[512]{0:T(512)S(1)}, /*index=5*/bf16[256,256]{1,0:T(8,128)(2,1)}, f32[512]{0:T(512)S(1)}, ...), branch_computations={%region_14.15_spmd, %region_15.20_spmd} | conditional | flops 408489472 | bytes 18143356 | solution.py:128
  92.0 1.0 fusion.100
  93.2 1.0 fusion.101
  94.5 0.6 fusion.32
  95.1 1.2 fusion.11
  97.1 1.9 fusion.31
  99.0 0.9 fusion.38
  100.4 1.3 fusion.30
  101.9 0.9 pad_maximum_fusion
  102.9 0.8 copy-done.1
  103.7 14.7 %reduce-scatter.3.cloned.1.call-done = f32[128,512]{0,1:T(8,128)} async-done(((f32[256,512]{0,1:T(8,128)}), f32[128,512]{0,1:T(8,128)}) %reduce-scatter.3.cloned.1.call-update) | async-done | bytes 262160 | tf_op jit(solution)/shard_map/reduce_scatter | solution.py:196
  118.4 5.4 %convolution_bitcast_fusion = f32[4096,512]{0,1:T(8,128)} fusion(bf16[1,128,4096]{2,1,0:T(8,128)(2,1)S(1)} %copy-done, f32[128,512]{0,1:T(8,128)} %reduce-scatter.3.cloned.1.call-done), kind=kOutput, calls=%fused_computation.135 | convolution fusion | flops 536936448 | bytes 9699328 | tf_op jit(solution)/shard_map/dot_general | solution.py:21
  123.9 99.3 %reduce-scatter.5.cloned.1.call-done = f32[2048,512]{0,1:T(8,128)} async-done(((f32[4096,512]{0,1:T(8,128)}), f32[2048,512]{0,1:T(8,128)}) %reduce-scatter.5.cloned.1.call-update) | async-done | bytes 4194320 | tf_op jit(solution)/shard_map/reduce_scatter | solution.py:207
  223.2 5.3 %copy.8 = f32[2048,2,256]{2,0,1:T(8,128)} copy(f32[2048,2,256]{0,2,1:T(8,128)} %bitcast.102) | data formatting | bytes 8388608 | tf_op jit(solution)/shard_map/reshape | solution.py:209
  228.6 155.2 %all-reduce.2.cloned.1.call-done = f32[2,2048,256]{2,1,0:T(8,128)} async-done(((f32[2,2048,256]{2,1,0:T(8,128)}), f32[2,2048,256]{2,1,0:T(8,128)}) %all-reduce.2.cloned.1.call-update) | async-done | bytes 4194320 | tf_op jit(solution)/shard_map/psum | solution.py:208
  383.7 6.0 %convert_multiply_fusion.4 = f32[2,2048,256]{2,1,0:T(8,128)} fusion(f32[2,2048,256]{2,1,0:T(8,128)} %all-reduce.2.cloned.1.call-done, s32[2,4096,256]{2,1,0:T(8,128)} %param.21, s32[]{:T(128)S(6)} %select_n.61), kind=kLoop, calls=%fused_computation.136 | loop fusion | flops 2097152 | bytes 12582916 | tf_op jit(solution)/shard_map/mul | solution.py:213
  (86 shorter events, 6.7 us)
Async XLA Ops:
  6.5 6.8 %copy-start = (bf16[1,128,4096]{2,1,0:T(8,128)(2,1)S(1)}, bf16[1,128,4096]{2,1,0:T(8,128)(2,1)}, u32[]{:S(2)}) copy-start(bf16[1,128,4096]{2,1,0:T(8,128)(2,1)} %param.16) | copy-start | bytes 3145732
  6.5 39.6 %all-gather.5.cloned.1.call-start = ((), (), s32[]{:S(2)}) async-start(), calls=%async_computation.3 | async-start | bytes 3145728 | tf_op jit(solution)/shard_map/all_gather | solution.py:154
  7.3 73.6 %all-gather.3.cloned.1.call-start = ((), (), s32[]{:S(2)}) async-start(), calls=%async_computation.2 | async-start | bytes 3145728 | tf_op jit(solution)/shard_map/all_gather | solution.py:149
  8.0 110.4 %reduce-scatter.3.cloned.1.call-start = ((), (), s32[]{:S(2)}) async-start(), calls=%async_computation.4 | async-start | bytes 786432 | tf_op jit(solution)/shard_map/reduce_scatter | solution.py:196
  19.6 63.3 %copy-start.2 = (bf16[256,256]{1,0:T(8,128)(2,1)}, bf16[256,256]{1,0:T(8,128)(2,1)S(1)}, u32[]{:S(2)}) copy-start(bf16[256,256]{1,0:T(8,128)(2,1)S(1)} %all_gather.20) | copy-start | bytes 393220
  26.4 61.5 %copy-start.4 = (bf16[256,256]{1,0:T(8,128)(2,1)}, bf16[256,256]{1,0:T(8,128)(2,1)S(1)}, u32[]{:S(2)}) copy-start(bf16[256,256]{1,0:T(8,128)(2,1)S(1)} %all_gather.23) | copy-start | bytes 393220
  53.1 35.1 %copy-start.6 = (bf16[256,256]{1,0:T(8,128)(2,1)}, bf16[256,256]{1,0:T(8,128)(2,1)S(1)}, u32[]{:S(2)}) copy-start(bf16[256,256]{1,0:T(8,128)(2,1)S(1)} %all_gather.22) | copy-start | bytes 393220
  87.8 0.7 copy-start.7
  93.2 3.4 copy-start.3
  94.4 1.8 copy-start.8
  94.5 2.4 copy-start.5
  99.9 2.0 copy-start.9
  102.9 0.8 copy-start.1
  103.7 119.5 %reduce-scatter.5.cloned.1.call-start = ((), (), s32[]{:S(2)}) async-start(), calls=%async_computation.5 | async-start | bytes 12582912 | tf_op jit(solution)/shard_map/reduce_scatter | solution.py:207
  123.8 259.9 %all-reduce.2.cloned.1.call-start = ((), (), s32[]{:S(2)}) async-start(), calls=%async_computation.6 | async-start | bytes 8388608 | tf_op jit(solution)/shard_map/psum | solution.py:208
Sparse Core Ops, SparseCore 0:
  8.9 37.2 all-gather.4
  47.7 33.1 all-gather.2
  103.8 14.5 reduce-scatter.2
  123.9 99.2 reduce-scatter.4
  228.7 154.9 all-reduce.1
where the time goes:
time: 397 us; the launch traced here: 396 us
  waiting for transfers between devices  318 us (80%)
  blocking collectives  22 us (6%)
  matrix products  20.4 us (5%)
  between operations  13.4 us (3%)
  other arithmetic  11.8 us (3%)
  local copies, waits for them, and re-layouts  10.1 us (3%)
    psum x1, waiting for transfers between devices, local(): hvp = lax.psum(partial_hvp, 'rep')  155 us
    reduce_scatter x1, waiting for transfers between devices, local(): lax.psum_scatter(times_tn(columns, grads), 'ctx', scatter_dimension=0, ti...  99.3 us
    all_gather x1, waiting for transfers between devices, local(): lax.all_gather(key_weight, 'ctx', axis=0, tiled=True)  27.7 us
    all_gather x1, waiting for transfers between devices, local(): lax.all_gather(value_weight, 'ctx', axis=0, tiled=True)  19.7 us
    reduce_scatter x1, waiting for transfers between devices, local(): lax.psum_scatter(pair_terms(query_local, cot_local, stats, query_start, k...  14.7 us
    dot_general x5, matrix products, times_tn(): lax.dot_general(left, right, (((0,), (0,)), ((), ())), preferred_element_...  9.7 us
  transfers between devices with their start and end apart: 5, of which 5 were waited for; matrix products, arithmetic and copies ran while one was open for 2% of the time, Pallas kernels for 0%

commit v1 on v0

--- a/solution.py
+++ b/solution.py
@@ -1,6 +1,10 @@
+import functools
+
 import jax
 import jax.numpy as jnp
 from jax import lax
+from jax.experimental import pallas as pl
+from jax.experimental.pallas import tpu as pltpu
 from jax.sharding import PartitionSpec as P
 
 HEADS = 32
@@ -10,6 +14,11 @@
 
 NEG_FILL = -1e30
 
+BF16 = jnp.bfloat16
+F32 = jnp.float32
+CHUNKS = 4
+N_REMOTE = 30
+
 
 def times_t(left, right):
     return lax.dot_general(
@@ -20,6 +29,293 @@
 def times_tn(left, right):
     return lax.dot_general(
         left, right, (((0,), (0,)), ((), ())), preferred_element_type=jnp.float32
+    )
+
+
+def fused_kernel(tok, q, cot, kw, vw, probe, out,
+                 gath, toks, qs, cots, kws, vws, signs, tan_own, tan_all,
+                 part_own, part_in, grads, acc,
+                 send_sem, recv_sem, local_sem, probe_sem, out_sem):
+    x = lax.axis_index("ctx")
+    h = lax.axis_index("head")
+    z = lax.axis_index("rep")
+    half = gath.shape[-1]
+    rows = qs.shape[1]
+    other = 1 - x
+    sib = h + 1 - 2 * lax.rem(h, 2)
+    yn = lax.rem(h + 2, 4)
+    sib_yn = lax.rem(sib + 2, 4)
+    zs = (z + 1 - 2 * lax.rem(z, 2), lax.rem(z + 2, 4), 3 - z)
+    to_x = (other, h, z)
+    to_s = (x, sib, z)
+    to_y = (x, yn, z)
+    to_z = tuple((x, h, zd) for zd in zs)
+
+    def cols(index, width):
+        return pl.ds(pl.multiple_of(index * width, width), width)
+
+    loads = [
+        pltpu.make_async_copy(tok, toks, local_sem.at[0]),
+        pltpu.make_async_copy(tok.at[:, :, cols(x, half)], gath.at[z, :, x], local_sem.at[1]),
+        pltpu.make_async_copy(kw, kws, local_sem.at[2]),
+        pltpu.make_async_copy(vw, vws, local_sem.at[3]),
+        pltpu.make_async_copy(q.at[:, cols(x, 512)], qs.at[x], local_sem.at[4]),
+        pltpu.make_async_copy(cot.at[:, cols(x, 512)], cots.at[x], local_sem.at[5]),
+    ]
+    step = 2 * half // CHUNKS
+    probes = [
+        [
+            pltpu.make_async_copy(
+                probe.at[t, pl.ds(c * step, step)],
+                signs.at[t, pl.ds(c * step, step)],
+                probe_sem.at[t * CHUNKS + c],
+            )
+            for c in range(CHUNKS)
+        ]
+        for t in range(2)
+    ]
+    loads[0].start()
+    for t in range(2):
+        for c in range(CHUNKS):
+            probes[t][c].start()
+    for load in loads[1:]:
+        load.start()
+
+    barrier = pltpu.get_barrier_semaphore()
+    for device in (to_x, to_s, to_y) + to_z:
+        pl.semaphore_signal(barrier, inc=1, device_id=device, device_id_type=pl.DeviceIdType.MESH)
+    pl.semaphore_wait(barrier, 6)
+
+    sent = []
+
+    def send(index, src, dst, device):
+        copy = pltpu.make_async_remote_copy(
+            src_ref=src, dst_ref=dst, send_sem=send_sem.at[index], recv_sem=recv_sem.at[index],
+            device_id=device, device_id_type=pl.DeviceIdType.MESH,
+        )
+        copy.start()
+        sent.append(copy)
+
+    def arrive(index, slot, device):
+        pltpu.make_async_remote_copy(
+            src_ref=slot, dst_ref=slot, send_sem=send_sem.at[index], recv_sem=recv_sem.at[index],
+            device_id=device, device_id_type=pl.DeviceIdType.MESH,
+        ).wait_recv()
+
+    send(0, tok.at[h, :, cols(other, half)], gath.at[z, h, x], to_x)
+    for d in range(3):
+        send(1 + d, tok.at[h, :, cols(x, half)], gath.at[z, h, x], to_z[d])
+    send(19, q.at[:, cols(other, 512)], qs.at[x], to_x)
+    send(20, cot.at[:, cols(other, 512)], cots.at[x], to_x)
+
+    def project_tangent(t):
+        total = jnp.zeros((rows, 256), F32)
+        for c in range(CHUNKS):
+            probes[t][c].wait()
+            sign = signs[t, pl.ds(c * step, step), :].astype(F32).astype(BF16)
+            block = toks[:, :, pl.ds(c * step, step)].reshape(rows, step)
+            total = total + jnp.dot(block, sign, preferred_element_type=F32)
+        half_total = total.astype(BF16)
+        for j in range(2):
+            tan_own[j, :, :, t * 128:(t + 1) * 128] = half_total[:, j * 128:(j + 1) * 128].reshape(4, rows // 4, 128)
+
+    loads[0].wait()
+    project_tangent(0)
+    arrive(0, gath.at[z, h, other], to_x)
+    send(7, gath.at[z, h, other], gath.at[z, h, other], to_y)
+    send(8, gath.at[z, h, other], gath.at[z, h, other], to_s)
+    for d in range(3):
+        send(4 + d, gath.at[z, h, other], gath.at[z, h, other], to_z[d])
+    project_tangent(1)
+    send(21, tan_own.at[other], tan_all.at[:, x], to_x)
+    arrive(7, gath.at[z, yn, other], to_y)
+    send(9, gath.at[z, yn, other], gath.at[z, yn, other], to_s)
+    tan_all[:, pl.ds(x, 1)] = tan_own[x][:, None]
+    arrive(8, gath.at[z, sib, other], to_s)
+    arrive(9, gath.at[z, sib_yn, other], to_s)
+    for index in (1, 2, 3):
+        loads[index].wait()
+    seq = 2 * rows
+    mine = gath[z].reshape(seq, half)
+    for t, weight in enumerate((kws, vws)):
+        partial = jnp.dot(mine, weight[...], preferred_element_type=F32)
+        for j in range(2):
+            part_own[j, :, t * 128:(t + 1) * 128] = partial[:, j * 128:(j + 1) * 128]
+    send(22, part_own.at[other], part_in, to_x)
+
+    def pass_rep(d):
+        arrive(1 + d, gath.at[zs[d], h, x], to_z[d])
+        arrive(4 + d, gath.at[zs[d], h, other], to_z[d])
+        send(10 + d, gath.at[zs[d], h], gath.at[zs[d], h], to_y)
+        send(13 + d, gath.at[zs[d], h], gath.at[zs[d], h], to_s)
+
+    def pass_sibling(d):
+        arrive(10 + d, gath.at[zs[d], yn], to_y)
+        send(16 + d, gath.at[zs[d], yn], gath.at[zs[d], yn], to_s)
+
+    pass_rep(0)
+    pass_rep(1)
+    loads[4].wait()
+    loads[5].wait()
+    arrive(19, qs.at[other], to_x)
+    arrive(20, cots.at[other], to_x)
+    arrive(21, tan_all.at[:, other], to_x)
+    arrive(22, part_in, to_x)
+
+    both = (part_own[x] + part_in[...]).astype(BF16)
+    keys, values = both[:, :128], both[:, 128:]
+    tangents = tan_all[...].reshape(seq, 256)
+    tan_keys, tan_values = tangents[:, :128], tangents[:, 128:]
+    scaling = HEAD_DIM ** (-0.5)
+    quarter = rows // 4
+    slot = lax.broadcasted_iota(jnp.int32, (seq, seq), 1)
+    key_pos = (
+        lax.rem(lax.div(slot, quarter), 2) * rows
+        + lax.div(slot, 2 * quarter) * quarter
+        + lax.rem(slot, quarter)
+    )
+    valid = key_pos <= lax.broadcasted_iota(jnp.int32, (seq, seq), 0)
+    key_terms = jnp.zeros((seq, 128), F32)
+    value_terms = jnp.zeros((seq, 128), F32)
+    hooks = (lambda: pass_rep(2), lambda: pass_sibling(0), lambda: pass_sibling(1), lambda: None)
+    for g in range(4):
+        hooks[g]()
+        span = slice(g * 128, (g + 1) * 128)
+        query = qs[:, :, span].reshape(seq, 128)
+        cotan = cots[:, :, span].reshape(seq, 128)
+        scores = jnp.where(valid, scaling * times_t(query, keys), NEG_FILL)
+        tan_scores = scaling * times_t(query, tan_keys)
+        peak = jnp.max(scores, axis=1, keepdims=True)
+        expo = jnp.exp(scores - peak)
+        total = jnp.sum(expo, axis=1, keepdims=True)
+        mixed = expo * tan_scores
+        along = jnp.sum(mixed, axis=1, keepdims=True)
+        expo_half = expo.astype(BF16)
+        acc_value = jnp.dot(expo_half, values, preferred_element_type=F32)
+        acc_mixed = jnp.dot(mixed.astype(BF16), values, preferred_element_type=F32)
+        acc_tan = jnp.dot(expo_half, tan_values, preferred_element_type=F32)
+        inverse = 1.0 / total
+        shift_mean = along * inverse
+        tan_sum = acc_mixed - shift_mean * acc_value + acc_tan
+        cot_float = cotan.astype(F32)
+        delta = jnp.sum(cot_float * acc_value, axis=1, keepdims=True) * inverse
+        tan_delta = jnp.sum(cot_float * tan_sum, axis=1, keepdims=True) * inverse
+        probs = expo * inverse
+        tan_probs = probs * (tan_scores - shift_mean)
+        dprob = times_t(cotan, values)
+        tan_dprob = times_t(cotan, tan_values)
+        tan_dscore = tan_probs * (dprob - delta) + probs * (tan_dprob - tan_delta)
+        value_terms = value_terms + times_tn(tan_probs.astype(BF16), cotan)
+        key_terms = key_terms + times_tn(tan_dscore.astype(BF16), query)
+    own = cols(x, 128)
+    theirs = cols(other, 128)
+    grads[z, 0, :, own] = (scaling * key_terms).astype(BF16)
+    grads[z, 1, :, own] = value_terms.astype(BF16)
+    mine_at = grads.at[z, :, :, own]
+    for d in range(3):
+        send(24 + d, mine_at, mine_at, to_z[d])
+    send(23, mine_at, mine_at, to_x)
+    pass_sibling(2)
+    for d in range(3):
+        arrive(13 + d, gath.at[zs[d], sib], to_s)
+        arrive(16 + d, gath.at[zs[d], sib_yn], to_s)
+
+    block = 256
+    blocks = half // block
+
+    def product(rep, start, t):
+        left = gath[rep, :, :, :, pl.ds(start, block)].reshape(seq, block)
+        return times_tn(left, grads[rep, t])
+
+    def pass_grads(d):
+        at = grads.at[zs[d], :, :, own]
+        arrive(24 + d, at, to_z[d])
+        send(27 + d, at, at, to_x)
+
+    def add_rep(rep, first):
+        @pl.loop(0, blocks)
+        def _(i):
+            start = pl.multiple_of(i * block, block)
+            for t in range(2):
+                value = product(rep, start, t)
+                if not first:
+                    value = value + acc[t, pl.ds(start, block), :]
+                acc[t, pl.ds(start, block), :] = value
+
+    pass_grads(0)
+    arrive(23, grads.at[z, :, :, theirs], to_x)
+    add_rep(z, True)
+    pass_grads(1)
+    pass_grads(2)
+    arrive(27, grads.at[zs[0], :, :, theirs], to_x)
+    add_rep(zs[0], False)
+    arrive(28, grads.at[zs[1], :, :, theirs], to_x)
+    add_rep(zs[1], False)
+    arrive(29, grads.at[zs[2], :, :, theirs], to_x)
+
+    def write(i):
+        start = pl.multiple_of(i * block, block)
+        return pltpu.make_async_copy(
+            acc.at[:, pl.ds(start, block)], out.at[:, pl.ds(start, block)], out_sem.at[i]
+        )
+
+    @pl.loop(0, blocks)
+    def _(i):
+        start = pl.multiple_of(i * block, block)
+        for t in range(2):
+            value = product(zs[2], start, t) + acc[t, pl.ds(start, block), :]
+            sign_at = pl.multiple_of(x * half + i * block, block)
+            acc[t, pl.ds(start, block), :] = value * signs[t, pl.ds(sign_at, block), :].astype(F32)
+        write(i).start()
+
+    @pl.loop(0, blocks)
+    def _(i):
+        write(i).wait()
+
+    for copy in sent:
+        copy.wait_send()
+
+
+def fused(tokens, queries, cotangent, key_weight, value_weight, probe):
+    _, rows, depth = tokens.shape
+    half = key_weight.shape[0]
+    any_spec = pl.BlockSpec(memory_space=pl.ANY)
+    return pl.pallas_call(
+        fused_kernel,
+        out_shape=jax.ShapeDtypeStruct((2, half, 256), F32),
+        in_specs=[any_spec] * 6,
+        out_specs=any_spec,
+        scratch_shapes=[
+            pltpu.VMEM((4, 4, 2, rows // 4, half), BF16),
+            pltpu.VMEM((4, rows // 4, depth), BF16),
+            pltpu.VMEM((2, rows, 512), BF16),
+            pltpu.VMEM((2, rows, 512), BF16),
+            pltpu.VMEM((half, 256), BF16),
+            pltpu.VMEM((half, 256), BF16),
+            pltpu.VMEM((2, depth, 256), jnp.int32),
+            pltpu.VMEM((2, 4, rows // 4, 256), BF16),
+            pltpu.VMEM((4, 2, rows // 4, 256), BF16),
+            pltpu.VMEM((2, 2 * rows, 256), F32),
+            pltpu.VMEM((2 * rows, 256), F32),
+            pltpu.VMEM((4, 2, 2 * rows, 256), BF16),
+            pltpu.VMEM((2, half, 256), F32),
+            pltpu.SemaphoreType.DMA((N_REMOTE,)),
+            pltpu.SemaphoreType.DMA((N_REMOTE,)),
+            pltpu.SemaphoreType.DMA((6,)),
+            pltpu.SemaphoreType.DMA((2 * CHUNKS,)),
+            pltpu.SemaphoreType.DMA((half // 256,)),
+        ],
+        compiler_params=pltpu.CompilerParams(
+            collective_id=0, has_side_effects=True, vmem_limit_bytes=56 * 1024 * 1024
+        ),
+        cost_estimate=pl.CostEstimate(flops=6 * 10**9, bytes_accessed=20 * 10**6, transcendentals=2**18),
+    )(
+        tokens.reshape(4, rows // 4, depth),
+        queries[0],
+        cotangent[0],
+        key_weight,
+        value_weight,
+        probe,
     )
 
 
@@ -213,9 +509,28 @@
     return sign_rows * hvp
 
 
+def fits(mesh, tokens):
+    sizes = mesh.shape
+    return (
+        sizes["ctx"] == 2
+        and sizes["head"] == 4
+        and sizes["rep"] == 4
+        and tokens.shape[0] == 4
+        and tokens.shape[1] == 256
+        and tokens.shape[2] == 4096
+    )
+
+
 def solution(mesh):
+    def run(*arguments):
+        return mapped(mesh, fused if fits(mesh, arguments[0]) else local)(*arguments)
+
+    return run
+
+
+def mapped(mesh, body):
     return jax.shard_map(
-        local,
+        body,
         mesh=mesh,
         in_specs=(
             P("rep", "ctx", None),

time: 397 us -> 59.5 us (0.15)
  waiting for transfers between devices: 318 us -> 0 us
  Pallas kernels: 0 us -> 54.8 us
  blocking collectives: 22 us -> 0 us
  matrix products: 20.4 us -> 0 us
  between operations: 13.4 us -> 0.01 us
  other arithmetic: 11.8 us -> 0 us
  local copies, waits for them, and re-layouts: 10.1 us -> 4.47 us
    psum x1 -> x0, waiting for transfers between devices: 155 us -> none  [local(): hvp = lax.psum(partial_hvp, 'rep')]
    reduce_scatter x2 -> x0, waiting for transfers between devices: 114 us -> none  [the longest x1 99.3 us: local(): lax.psum_scatter(times_tn(columns, grads), 'ctx', scatter_dimension=0, ti...]
    pallas_call x0 -> x1, Pallas kernels: none -> 54.8 us  [fused(): pl.pallas_call(fused_kernel, out_shape=jax.ShapeDtypeStruct((2, half, 256...]
    all_gather x2 -> x0, waiting for transfers between devices: 47.4 us -> none  [the longest x1 27.7 us: local(): lax.all_gather(key_weight, 'ctx', axis=0, tiled=True)]
    all_gather x4 -> x0, blocking collectives: 22 us -> none  [the longest x1 6.31 us: local(): lax.all_gather(own_tan_values, 'ctx', axis=0, tiled=True)]
    dot_general x27 -> x0, matrix products: 20.4 us -> none  [the longest x5 9.7 us: times_tn(): lax.dot_general(left, right, (((0,), (0,)), ((), ())), preferred_element_...]
    mul x1 -> x0, other arithmetic: 6.02 us -> none  [local(): return sign_rows * hvp]
    reshape x7 -> x0, local copies, waits for them, and re-layouts: 5.87 us -> none  [the longest x1 5.34 us: local(): hvp = hvp.reshape(own_rows, 2, width).transpose(1, 0, 2)]
  transfers between devices with their start and end apart: 5 -> 0, of which waited for: 5 -> 0; matrix products, arithmetic and copies ran while one was open for 2% -> 0% of each run, Pallas kernels for 0% -> 0%
where the time goes in v1:
time: 59.5 us; the launch traced here: 59.3 us
  Pallas kernels  54.8 us (92%)
  local copies, waits for them, and re-layouts  4.47 us (8%)
    pallas_call x1, Pallas kernels, fused(): pl.pallas_call(fused_kernel, out_shape=jax.ShapeDtypeStruct((2, half, 256...  54.8 us
    unnamed x1, local copies, waits for them, and re-layouts  4.47 us

profile of v1, /device:TPU:0, one launch (start us, length us, event | category | flops | bytes accessed | tf_op | source)
XLA Modules:
  0.0 59.3 jit_solution(1330561688599120657)
XLA Ops:
  0.0 54.8 %shard_map.64 = f32[2,2048,256]{2,1,0:T(8,128)} custom-call(bf16[4,32,4096]{2,1,0:T(8,128)(2,1)} %bitcast.3, bf16[128,1024]{1,0:T(8,128)(2,1)} %bitcast.4, bf16[128,1024]{1,0:T(8,128)(2,1)} %bitcast.5, bf16[2048,256]{1,0:T(8,128)(2,1)} %kw.1, bf16[2048,256]{1,0:T(8,128)(2,1)} %vw.1, s32[2,4096,256]{2,1,0:T(8,128)} %probe.1), custom_call_target="tpu_custom_call" | custom-call | flops 6000000000 | bytes 20000000 | tf_op jit(solution)/shard_map/pallas_call | solution.py:283
  54.9 4.5 %copy.8 = f32[2,2048,256]{2,1,0:T(8,128)} copy(f32[2,2048,256]{2,1,0:T(8,128)} %shard_map.64) | data formatting | bytes 8388608

commit v2 on v1

--- a/solution.py
+++ b/solution.py
@@ -17,7 +17,7 @@
 BF16 = jnp.bfloat16
 F32 = jnp.float32
 CHUNKS = 4
-N_REMOTE = 30
+N_REMOTE = 40
 
 
 def times_t(left, right):
@@ -74,12 +74,13 @@
         ]
         for t in range(2)
     ]
-    loads[0].start()
+    for index in (0, 2, 3, 1):
+        loads[index].start()
     for t in range(2):
         for c in range(CHUNKS):
             probes[t][c].start()
-    for load in loads[1:]:
-        load.start()
+    for index in (4, 5):
+        loads[index].start()
 
     barrier = pltpu.get_barrier_semaphore()
     for device in (to_x, to_s, to_y) + to_z:
@@ -119,7 +120,18 @@
         for j in range(2):
             tan_own[j, :, :, t * 128:(t + 1) * 128] = half_total[:, j * 128:(j + 1) * 128].reshape(4, rows // 4, 128)
 
-    loads[0].wait()
+    def project_rows(block, ctx):
+        for t, weight in enumerate((kws, vws)):
+            partial = jnp.dot(block.reshape(rows, half), weight[...], preferred_element_type=F32)
+            for j in range(2):
+                part_own[j, :, pl.ds(ctx, 1), :, t * 128:(t + 1) * 128] = (
+                    partial[:, j * 128:(j + 1) * 128].reshape(4, 1, rows // 4, 128)
+                )
+
+    for index in (0, 2, 3):
+        loads[index].wait()
+    project_rows(toks[:, :, cols(x, half)], x)
+    send(22, part_own.at[other, :, x], part_in.at[:, x], to_x)
     project_tangent(0)
     arrive(0, gath.at[z, h, other], to_x)
     send(7, gath.at[z, h, other], gath.at[z, h, other], to_y)
@@ -128,41 +140,44 @@
         send(4 + d, gath.at[z, h, other], gath.at[z, h, other], to_z[d])
     project_tangent(1)
     send(21, tan_own.at[other], tan_all.at[:, x], to_x)
+    tan_all[:, pl.ds(x, 1)] = tan_own[x][:, None]
+    arrive(8, gath.at[z, sib, other], to_s)
     arrive(7, gath.at[z, yn, other], to_y)
     send(9, gath.at[z, yn, other], gath.at[z, yn, other], to_s)
-    tan_all[:, pl.ds(x, 1)] = tan_own[x][:, None]
-    arrive(8, gath.at[z, sib, other], to_s)
     arrive(9, gath.at[z, sib_yn, other], to_s)
-    for index in (1, 2, 3):
-        loads[index].wait()
     seq = 2 * rows
-    mine = gath[z].reshape(seq, half)
-    for t, weight in enumerate((kws, vws)):
-        partial = jnp.dot(mine, weight[...], preferred_element_type=F32)
-        for j in range(2):
-            part_own[j, :, t * 128:(t + 1) * 128] = partial[:, j * 128:(j + 1) * 128]
-    send(22, part_own.at[other], part_in, to_x)
-
-    def pass_rep(d):
-        arrive(1 + d, gath.at[zs[d], h, x], to_z[d])
-        arrive(4 + d, gath.at[zs[d], h, other], to_z[d])
-        send(10 + d, gath.at[zs[d], h], gath.at[zs[d], h], to_y)
-        send(13 + d, gath.at[zs[d], h], gath.at[zs[d], h], to_s)
-
-    def pass_sibling(d):
-        arrive(10 + d, gath.at[zs[d], yn], to_y)
-        send(16 + d, gath.at[zs[d], yn], gath.at[zs[d], yn], to_s)
-
-    pass_rep(0)
-    pass_rep(1)
+    project_rows(gath[z, :, other], other)
+    send(39, part_own.at[other, :, other], part_in.at[:, other], to_x)
+
+    ctxs = (x, other)
+    from_z = ((1, 2, 3), (4, 5, 6))
+    from_y = ((10, 11, 12), (30, 31, 32))
+    from_s = ((13, 14, 15), (33, 34, 35))
+    from_sy = ((16, 17, 18), (36, 37, 38))
+
+    def pass_rep(part, d):
+        at = gath.at[zs[d], h, ctxs[part]]
+        arrive(from_z[part][d], at, to_z[d])
+        send(from_y[part][d], at, at, to_y)
+        send(from_s[part][d], at, at, to_s)
+
+    def pass_sibling(part, d):
+        at = gath.at[zs[d], yn, ctxs[part]]
+        arrive(from_y[part][d], at, to_y)
+        send(from_sy[part][d], at, at, to_s)
+
+    for d in range(3):
+        pass_rep(0, d)
+    loads[1].wait()
     loads[4].wait()
     loads[5].wait()
     arrive(19, qs.at[other], to_x)
     arrive(20, cots.at[other], to_x)
     arrive(21, tan_all.at[:, other], to_x)
-    arrive(22, part_in, to_x)
-
-    both = (part_own[x] + part_in[...]).astype(BF16)
+    arrive(22, part_in.at[:, other], to_x)
+    arrive(39, part_in.at[:, x], to_x)
+
+    both = (part_own[x] + part_in[...]).reshape(seq, 256).astype(BF16)
     keys, values = both[:, :128], both[:, 128:]
     tangents = tan_all[...].reshape(seq, 256)
     tan_keys, tan_values = tangents[:, :128], tangents[:, 128:]
@@ -177,9 +192,7 @@
     valid = key_pos <= lax.broadcasted_iota(jnp.int32, (seq, seq), 0)
     key_terms = jnp.zeros((seq, 128), F32)
     value_terms = jnp.zeros((seq, 128), F32)
-    hooks = (lambda: pass_rep(2), lambda: pass_sibling(0), lambda: pass_sibling(1), lambda: None)
     for g in range(4):
-        hooks[g]()
         span = slice(g * 128, (g + 1) * 128)
         query = qs[:, :, span].reshape(seq, 128)
         cotan = cots[:, :, span].reshape(seq, 128)
@@ -215,10 +228,10 @@
     for d in range(3):
         send(24 + d, mine_at, mine_at, to_z[d])
     send(23, mine_at, mine_at, to_x)
-    pass_sibling(2)
-    for d in range(3):
-        arrive(13 + d, gath.at[zs[d], sib], to_s)
-        arrive(16 + d, gath.at[zs[d], sib_yn], to_s)
+    for d in range(3):
+        pass_rep(1, d)
+    for d in range(3):
+        pass_sibling(0, d)
 
     block = 256
     blocks = half // block
@@ -242,16 +255,24 @@
                     value = value + acc[t, pl.ds(start, block), :]
                 acc[t, pl.ds(start, block), :] = value
 
+    def rest_of(d):
+        for part in range(2):
+            arrive(from_s[part][d], gath.at[zs[d], sib, ctxs[part]], to_s)
+            arrive(from_sy[part][d], gath.at[zs[d], sib_yn, ctxs[part]], to_s)
+        arrive(27 + d, grads.at[zs[d], :, :, theirs], to_x)
+
     pass_grads(0)
     arrive(23, grads.at[z, :, :, theirs], to_x)
     add_rep(z, True)
     pass_grads(1)
     pass_grads(2)
-    arrive(27, grads.at[zs[0], :, :, theirs], to_x)
+    for d in range(3):
+        pass_sibling(1, d)
+    rest_of(0)
     add_rep(zs[0], False)
-    arrive(28, grads.at[zs[1], :, :, theirs], to_x)
+    rest_of(1)
     add_rep(zs[1], False)
-    arrive(29, grads.at[zs[2], :, :, theirs], to_x)
+    rest_of(2)
 
     def write(i):
         start = pl.multiple_of(i * block, block)
@@ -295,8 +316,8 @@
             pltpu.VMEM((2, depth, 256), jnp.int32),
             pltpu.VMEM((2, 4, rows // 4, 256), BF16),
             pltpu.VMEM((4, 2, rows // 4, 256), BF16),
-            pltpu.VMEM((2, 2 * rows, 256), F32),
-            pltpu.VMEM((2 * rows, 256), F32),
+            pltpu.VMEM((2, 4, 2, rows // 4, 256), F32),
+            pltpu.VMEM((4, 2, rows // 4, 256), F32),
             pltpu.VMEM((4, 2, 2 * rows, 256), BF16),
             pltpu.VMEM((2, half, 256), F32),
             pltpu.SemaphoreType.DMA((N_REMOTE,)),

time: 59.5 us -> 53.7 us (0.903)
  Pallas kernels: 54.8 us -> 49.1 us
    pallas_call x1, Pallas kernels: 54.8 us -> 49.1 us  [fused(): pl.pallas_call(fused_kernel, out_shape=jax.ShapeDtypeStruct((2, half, 256...]
where the time goes in v2:
time: 53.7 us; the launch traced here: 53.5 us
  Pallas kernels  49.1 us (91%)
  local copies, waits for them, and re-layouts  4.47 us (8%)
    pallas_call x1, Pallas kernels, fused(): pl.pallas_call(fused_kernel, out_shape=jax.ShapeDtypeStruct((2, half, 256...  49.1 us
    unnamed x1, local copies, waits for them, and re-layouts  4.47 us

profile of v2, /device:TPU:0, one launch (start us, length us, event | category | flops | bytes accessed | tf_op | source)
XLA Modules:
  0.0 53.5 jit_solution(2156852292174702786)
XLA Ops:
  0.0 49.1 %shard_map.64 = f32[2,2048,256]{2,1,0:T(8,128)} custom-call(bf16[4,32,4096]{2,1,0:T(8,128)(2,1)} %bitcast.3, bf16[128,1024]{1,0:T(8,128)(2,1)} %bitcast.4, bf16[128,1024]{1,0:T(8,128)(2,1)} %bitcast.5, bf16[2048,256]{1,0:T(8,128)(2,1)} %kw.1, bf16[2048,256]{1,0:T(8,128)(2,1)} %vw.1, s32[2,4096,256]{2,1,0:T(8,128)} %probe.1), custom_call_target="tpu_custom_call" | custom-call | flops 6000000000 | bytes 20000000 | tf_op jit(solution)/shard_map/pallas_call | solution.py:304
  49.1 4.5 %copy.8 = f32[2,2048,256]{2,1,0:T(8,128)} copy(f32[2,2048,256]{2,1,0:T(8,128)} %shard_map.64) | data formatting | bytes 8388608

commit v3 on v2

--- a/solution.py
+++ b/solution.py
@@ -18,6 +18,7 @@
 F32 = jnp.float32
 CHUNKS = 4
 N_REMOTE = 40
+STORES = 8
 
 
 def times_t(left, right):
@@ -32,10 +33,10 @@
     )
 
 
-def fused_kernel(tok, q, cot, kw, vw, probe, out,
+def fused_kernel(tok, q, cot, kw, vw, probe, acc,
                  gath, toks, qs, cots, kws, vws, signs, tan_own, tan_all,
-                 part_own, part_in, grads, acc,
-                 send_sem, recv_sem, local_sem, probe_sem, out_sem):
+                 part_own, part_in, grads, flipped,
+                 send_sem, recv_sem, local_sem, probe_sem):
     x = lax.axis_index("ctx")
     h = lax.axis_index("head")
     z = lax.axis_index("rep")
@@ -166,9 +167,20 @@
         arrive(from_y[part][d], at, to_y)
         send(from_sy[part][d], at, at, to_s)
 
+    block = 256
+    blocks = half // block
+
+    def flip(rep):
+        @pl.loop(0, blocks)
+        def _(i):
+            start = pl.multiple_of(i * block, block)
+            left = gath[rep, :, :, :, pl.ds(start, block)].reshape(seq, block)
+            flipped[rep, pl.ds(start, block), :] = left.T
+
     for d in range(3):
         pass_rep(0, d)
     loads[1].wait()
+    flip(z)
     loads[4].wait()
     loads[5].wait()
     arrive(19, qs.at[other], to_x)
@@ -233,12 +245,8 @@
     for d in range(3):
         pass_sibling(0, d)
 
-    block = 256
-    blocks = half // block
-
     def product(rep, start, t):
-        left = gath[rep, :, :, :, pl.ds(start, block)].reshape(seq, block)
-        return times_tn(left, grads[rep, t])
+        return jnp.dot(flipped[rep, pl.ds(start, block), :], grads[rep, t], preferred_element_type=F32)
 
     def pass_grads(d):
         at = grads.at[zs[d], :, :, own]
@@ -255,30 +263,27 @@
                     value = value + acc[t, pl.ds(start, block), :]
                 acc[t, pl.ds(start, block), :] = value
 
-    def rest_of(d):
+    def flip_rest(d):
         for part in range(2):
             arrive(from_s[part][d], gath.at[zs[d], sib, ctxs[part]], to_s)
             arrive(from_sy[part][d], gath.at[zs[d], sib_yn, ctxs[part]], to_s)
-        arrive(27 + d, grads.at[zs[d], :, :, theirs], to_x)
+        flip(zs[d])
 
     pass_grads(0)
     arrive(23, grads.at[z, :, :, theirs], to_x)
     add_rep(z, True)
+    for d in range(3):
+        pass_sibling(1, d)
     pass_grads(1)
+    flip_rest(0)
     pass_grads(2)
-    for d in range(3):
-        pass_sibling(1, d)
-    rest_of(0)
+    flip_rest(1)
+    flip_rest(2)
+    arrive(27, grads.at[zs[0], :, :, theirs], to_x)
     add_rep(zs[0], False)
-    rest_of(1)
+    arrive(28, grads.at[zs[1], :, :, theirs], to_x)
     add_rep(zs[1], False)
-    rest_of(2)
-
-    def write(i):
-        start = pl.multiple_of(i * block, block)
-        return pltpu.make_async_copy(
-            acc.at[:, pl.ds(start, block)], out.at[:, pl.ds(start, block)], out_sem.at[i]
-        )
+    arrive(29, grads.at[zs[2], :, :, theirs], to_x)
 
     @pl.loop(0, blocks)
     def _(i):
@@ -287,25 +292,34 @@
             value = product(zs[2], start, t) + acc[t, pl.ds(start, block), :]
             sign_at = pl.multiple_of(x * half + i * block, block)
             acc[t, pl.ds(start, block), :] = value * signs[t, pl.ds(sign_at, block), :].astype(F32)
-        write(i).start()
-
-    @pl.loop(0, blocks)
-    def _(i):
-        write(i).wait()
 
     for copy in sent:
         copy.wait_send()
+
+
+def store_kernel(result, out, sem):
+    piece = result.shape[1] // STORES
+    copies = [
+        pltpu.make_async_copy(
+            result.at[:, pl.ds(i * piece, piece)], out.at[:, pl.ds(i * piece, piece)], sem.at[i]
+        )
+        for i in range(STORES)
+    ]
+    for copy in copies:
+        copy.start()
+    for copy in copies:
+        copy.wait()
 
 
 def fused(tokens, queries, cotangent, key_weight, value_weight, probe):
     _, rows, depth = tokens.shape
     half = key_weight.shape[0]
     any_spec = pl.BlockSpec(memory_space=pl.ANY)
-    return pl.pallas_call(
+    result = pl.pallas_call(
         fused_kernel,
-        out_shape=jax.ShapeDtypeStruct((2, half, 256), F32),
+        out_shape=pltpu.VMEM((2, half, 256), F32),
         in_specs=[any_spec] * 6,
-        out_specs=any_spec,
+        out_specs=pl.BlockSpec(memory_space=pltpu.VMEM),
         scratch_shapes=[
             pltpu.VMEM((4, 4, 2, rows // 4, half), BF16),
             pltpu.VMEM((4, rows // 4, depth), BF16),
@@ -319,25 +333,33 @@
             pltpu.VMEM((2, 4, 2, rows // 4, 256), F32),
             pltpu.VMEM((4, 2, rows // 4, 256), F32),
             pltpu.VMEM((4, 2, 2 * rows, 256), BF16),
-            pltpu.VMEM((2, half, 256), F32),
+            pltpu.VMEM((4, half, 2 * rows), BF16),
             pltpu.SemaphoreType.DMA((N_REMOTE,)),
             pltpu.SemaphoreType.DMA((N_REMOTE,)),
             pltpu.SemaphoreType.DMA((6,)),
             pltpu.SemaphoreType.DMA((2 * CHUNKS,)),
-            pltpu.SemaphoreType.DMA((half // 256,)),
         ],
         compiler_params=pltpu.CompilerParams(
             collective_id=0, has_side_effects=True, vmem_limit_bytes=56 * 1024 * 1024
         ),
         cost_estimate=pl.CostEstimate(flops=6 * 10**9, bytes_accessed=20 * 10**6, transcendentals=2**18),
     )(
-        tokens.reshape(4, rows // 4, depth),
-        queries[0],
-        cotangent[0],
-        key_weight,
-        value_weight,
+        pltpu.with_memory_space_constraint(tokens.reshape(4, rows // 4, depth), pltpu.HBM),
+        pltpu.with_memory_space_constraint(queries[0], pltpu.HBM),
+        pltpu.with_memory_space_constraint(cotangent[0], pltpu.HBM),
+        pltpu.with_memory_space_constraint(key_weight, pltpu.HBM),
+        pltpu.with_memory_space_constraint(value_weight, pltpu.HBM),
         probe,
     )
+    return pl.pallas_call(
+        store_kernel,
+        out_shape=jax.ShapeDtypeStruct(result.shape, F32),
+        in_specs=[pl.BlockSpec(memory_space=pltpu.VMEM)],
+        out_specs=any_spec,
+        scratch_shapes=[pltpu.SemaphoreType.DMA((STORES,))],
+        compiler_params=pltpu.CompilerParams(vmem_limit_bytes=4 * 1024 * 1024),
+        cost_estimate=pl.CostEstimate(flops=0, bytes_accessed=8 * 10**6, transcendentals=0),
+    )(result)
 
 
 def head_rows(block, head_index, group):

time: 53.7 us -> 49.6 us (0.924)
  local copies, waits for them, and re-layouts: 4.47 us -> 0 us
    unnamed x1 -> x0, local copies, waits for them, and re-layouts: 4.47 us -> none
    pallas_call x1 -> x2, Pallas kernels: 49.1 us -> 49.4 us  [the longest x1 47.3 us: fused(): pl.pallas_call(fused_kernel, out_shape=pltpu.VMEM((2, half, 256), F32), i...]
where the time goes in v3:
time: 49.6 us; the launch traced here: 49.4 us
  Pallas kernels  49.4 us (100%)
    pallas_call x1, Pallas kernels, fused(): pl.pallas_call(fused_kernel, out_shape=pltpu.VMEM((2, half, 256), F32), i...  47.3 us
    pallas_call x1, Pallas kernels, fused(): pl.pallas_call(store_kernel, out_shape=jax.ShapeDtypeStruct(result.shape,...  2.07 us

profile of v3, /device:TPU:0, one launch (start us, length us, event | category | flops | bytes accessed | tf_op | source)
XLA Modules:
  0.0 49.4 jit_solution(616395889016828869)
XLA Ops:
  0.0 47.3 %shard_map.64.result = f32[2,2048,256]{2,1,0:T(8,128)S(1)} custom-call(bf16[4,32,4096]{2,1,0:T(8,128)(2,1)} %bitcast.3, bf16[128,1024]{1,0:T(8,128)(2,1)} %bitcast.4, bf16[128,1024]{1,0:T(8,128)(2,1)} %bitcast.5, bf16[2048,256]{1,0:T(8,128)(2,1)} %kw.1, bf16[2048,256]{1,0:T(8,128)(2,1)} %vw.1, s32[2,4096,256]{2,1,0:T(8,128)} %probe.1), custom_call_target="tpu_custom_call" | custom-call | flops 6000000000 | bytes 20000000 | tf_op jit(solution)/shard_map/pallas_call | solution.py:318
  47.4 2.1 %shard_map.65 = f32[2,2048,256]{2,1,0:T(8,128)} custom-call(f32[2,2048,256]{2,1,0:T(8,128)S(1)} %shard_map.64.result), custom_call_target="tpu_custom_call" | custom-call | bytes 8000000 | tf_op jit(solution)/shard_map/pallas_call | solution.py:354

commit v4 on v3

--- a/solution.py
+++ b/solution.py
@@ -17,7 +17,7 @@
 BF16 = jnp.bfloat16
 F32 = jnp.float32
 CHUNKS = 4
-N_REMOTE = 40
+N_REMOTE = 43
 STORES = 8
 
 
@@ -87,16 +87,36 @@
     for device in (to_x, to_s, to_y) + to_z:
         pl.semaphore_signal(barrier, inc=1, device_id=device, device_id_type=pl.DeviceIdType.MESH)
     pl.semaphore_wait(barrier, 6)
+    inner = (z - 1) * (z - 2) == 0
 
     sent = []
-
-    def send(index, src, dst, device):
-        copy = pltpu.make_async_remote_copy(
-            src_ref=src, dst_ref=dst, send_sem=send_sem.at[index], recv_sem=recv_sem.at[index],
+    sent_inner = []
+
+    def describe(index, src, dst, device, land=None):
+        return pltpu.make_async_remote_copy(
+            src_ref=src, dst_ref=dst, send_sem=send_sem.at[index],
+            recv_sem=recv_sem.at[index if land is None else land],
             device_id=device, device_id_type=pl.DeviceIdType.MESH,
         )
-        copy.start()
-        sent.append(copy)
+
+    def send_all(*arguments):
+        describe(*arguments).start()
+        sent.append(arguments)
+
+    def send_inner(*arguments):
+        sent_inner.append(arguments)
+
+        @pl.when(inner)
+        def _():
+            describe(*arguments).start()
+
+    def send_rep(first, src, dst):
+        send_all(first + 1, src, dst, to_z[1])
+        send_inner(first + 2, src, dst, to_z[2])
+        send_all(first, src, dst, to_z[0])
+
+    def relay(index, at, land):
+        send_inner(index, at, at, to_z[0], land)
 
     def arrive(index, slot, device):
         pltpu.make_async_remote_copy(
@@ -104,11 +124,10 @@
             device_id=device, device_id_type=pl.DeviceIdType.MESH,
         ).wait_recv()
 
-    send(0, tok.at[h, :, cols(other, half)], gath.at[z, h, x], to_x)
-    for d in range(3):
-        send(1 + d, tok.at[h, :, cols(x, half)], gath.at[z, h, x], to_z[d])
-    send(19, q.at[:, cols(other, 512)], qs.at[x], to_x)
-    send(20, cot.at[:, cols(other, 512)], cots.at[x], to_x)
+    send_all(0, tok.at[h, :, cols(other, half)], gath.at[z, h, x], to_x)
+    send_rep(1, tok.at[h, :, cols(x, half)], gath.at[z, h, x])
+    send_all(19, q.at[:, cols(other, 512)], qs.at[x], to_x)
+    send_all(20, cot.at[:, cols(other, 512)], cots.at[x], to_x)
 
     def project_tangent(t):
         total = jnp.zeros((rows, 256), F32)
@@ -132,23 +151,22 @@
     for index in (0, 2, 3):
         loads[index].wait()
     project_rows(toks[:, :, cols(x, half)], x)
-    send(22, part_own.at[other, :, x], part_in.at[:, x], to_x)
+    send_all(22, part_own.at[other, :, x], part_in.at[:, x], to_x)
     project_tangent(0)
     arrive(0, gath.at[z, h, other], to_x)
-    send(7, gath.at[z, h, other], gath.at[z, h, other], to_y)
-    send(8, gath.at[z, h, other], gath.at[z, h, other], to_s)
-    for d in range(3):
-        send(4 + d, gath.at[z, h, other], gath.at[z, h, other], to_z[d])
+    send_all(7, gath.at[z, h, other], gath.at[z, h, other], to_y)
+    send_all(8, gath.at[z, h, other], gath.at[z, h, other], to_s)
+    send_rep(4, gath.at[z, h, other], gath.at[z, h, other])
     project_tangent(1)
-    send(21, tan_own.at[other], tan_all.at[:, x], to_x)
+    send_all(21, tan_own.at[other], tan_all.at[:, x], to_x)
     tan_all[:, pl.ds(x, 1)] = tan_own[x][:, None]
     arrive(8, gath.at[z, sib, other], to_s)
     arrive(7, gath.at[z, yn, other], to_y)
-    send(9, gath.at[z, yn, other], gath.at[z, yn, other], to_s)
+    send_all(9, gath.at[z, yn, other], gath.at[z, yn, other], to_s)
     arrive(9, gath.at[z, sib_yn, other], to_s)
     seq = 2 * rows
     project_rows(gath[z, :, other], other)
-    send(39, part_own.at[other, :, other], part_in.at[:, other], to_x)
+    send_all(39, part_own.at[other, :, other], part_in.at[:, other], to_x)
 
     ctxs = (x, other)
     from_z = ((1, 2, 3), (4, 5, 6))
@@ -159,13 +177,15 @@
     def pass_rep(part, d):
         at = gath.at[zs[d], h, ctxs[part]]
         arrive(from_z[part][d], at, to_z[d])
-        send(from_y[part][d], at, at, to_y)
-        send(from_s[part][d], at, at, to_s)
+        if d == 1:
+            relay(40 + part, at, from_z[part][2])
+        send_all(from_y[part][d], at, at, to_y)
+        send_all(from_s[part][d], at, at, to_s)
 
     def pass_sibling(part, d):
         at = gath.at[zs[d], yn, ctxs[part]]
         arrive(from_y[part][d], at, to_y)
-        send(from_sy[part][d], at, at, to_s)
+        send_all(from_sy[part][d], at, at, to_s)
 
     block = 256
     blocks = half // block
@@ -177,7 +197,7 @@
             left = gath[rep, :, :, :, pl.ds(start, block)].reshape(seq, block)
             flipped[rep, pl.ds(start, block), :] = left.T
 
-    for d in range(3):
+    for d in (1, 0, 2):
         pass_rep(0, d)
     loads[1].wait()
     flip(z)
@@ -205,6 +225,8 @@
     key_terms = jnp.zeros((seq, 128), F32)
     value_terms = jnp.zeros((seq, 128), F32)
     for g in range(4):
+        if g:
+            pass_rep(1, (1, 0, 2)[g - 1])
         span = slice(g * 128, (g + 1) * 128)
         query = qs[:, :, span].reshape(seq, 128)
         cotan = cots[:, :, span].reshape(seq, 128)
@@ -237,11 +259,8 @@
     grads[z, 0, :, own] = (scaling * key_terms).astype(BF16)
     grads[z, 1, :, own] = value_terms.astype(BF16)
     mine_at = grads.at[z, :, :, own]
-    for d in range(3):
-        send(24 + d, mine_at, mine_at, to_z[d])
-    send(23, mine_at, mine_at, to_x)
-    for d in range(3):
-        pass_rep(1, d)
+    send_rep(24, mine_at, mine_at)
+    send_all(23, mine_at, mine_at, to_x)
     for d in range(3):
         pass_sibling(0, d)
 
@@ -251,7 +270,9 @@
     def pass_grads(d):
         at = grads.at[zs[d], :, :, own]
         arrive(24 + d, at, to_z[d])
-        send(27 + d, at, at, to_x)
+        if d == 1:
+            relay(42, at, 26)
+        send_all(27 + d, at, at, to_x)
 
     def add_rep(rep, first):
         @pl.loop(0, blocks)
@@ -269,15 +290,15 @@
             arrive(from_sy[part][d], gath.at[zs[d], sib_yn, ctxs[part]], to_s)
         flip(zs[d])
 
+    pass_grads(1)
+    arrive(23, grads.at[z, :, :, theirs], to_x)
     pass_grads(0)
-    arrive(23, grads.at[z, :, :, theirs], to_x)
     add_rep(z, True)
-    for d in range(3):
+    for d in (1, 0, 2):
         pass_sibling(1, d)
-    pass_grads(1)
+    flip_rest(1)
+    pass_grads(2)
     flip_rest(0)
-    pass_grads(2)
-    flip_rest(1)
     flip_rest(2)
     arrive(27, grads.at[zs[0], :, :, theirs], to_x)
     add_rep(zs[0], False)
@@ -293,8 +314,13 @@
             sign_at = pl.multiple_of(x * half + i * block, block)
             acc[t, pl.ds(start, block), :] = value * signs[t, pl.ds(sign_at, block), :].astype(F32)
 
-    for copy in sent:
-        copy.wait_send()
+    for arguments in sent:
+        describe(*arguments).wait_send()
+
+    @pl.when(inner)
+    def _():
+        for arguments in sent_inner:
+            describe(*arguments).wait_send()
 
 
 def store_kernel(result, out, sem):

time: 49.6 us -> 47.9 us (0.966)
  Pallas kernels: 49.4 us -> 47.3 us
    pallas_call x1, Pallas kernels: 47.3 us -> 45.2 us  [fused(): pl.pallas_call(fused_kernel, out_shape=pltpu.VMEM((2, half, 256), F32), i...]
where the time goes in v4:
time: 47.9 us; the launch traced here: 47.3 us
  Pallas kernels  47.3 us (99%)
    pallas_call x1, Pallas kernels, fused(): pl.pallas_call(fused_kernel, out_shape=pltpu.VMEM((2, half, 256), F32), i...  45.2 us
    pallas_call x1, Pallas kernels, fused(): pl.pallas_call(store_kernel, out_shape=jax.ShapeDtypeStruct(result.shape,...  2.07 us

profile of v4, /device:TPU:0, one launch (start us, length us, event | category | flops | bytes accessed | tf_op | source)
XLA Modules:
  0.0 47.3 jit_solution(964486421413472448)
XLA Ops:
  0.0 45.2 %shard_map.64.result = f32[2,2048,256]{2,1,0:T(8,128)S(1)} custom-call(bf16[4,32,4096]{2,1,0:T(8,128)(2,1)} %bitcast.3, bf16[128,1024]{1,0:T(8,128)(2,1)} %bitcast.4, bf16[128,1024]{1,0:T(8,128)(2,1)} %bitcast.5, bf16[2048,256]{1,0:T(8,128)(2,1)} %kw.1, bf16[2048,256]{1,0:T(8,128)(2,1)} %vw.1, s32[2,4096,256]{2,1,0:T(8,128)} %probe.1), custom_call_target="tpu_custom_call" | custom-call | flops 6000000000 | bytes 20000000 | tf_op jit(solution)/shard_map/pallas_call | solution.py:344
  45.3 2.1 %shard_map.65 = f32[2,2048,256]{2,1,0:T(8,128)} custom-call(f32[2,2048,256]{2,1,0:T(8,128)S(1)} %shard_map.64.result), custom_call_target="tpu_custom_call" | custom-call | bytes 8000000 | tf_op jit(solution)/shard_map/pallas_call | solution.py:380
